TPU v7x, 32 devices: a whole 2x2x4 slice. The times are simulated.
32 devices in a mesh: rows: 16 (over z, y, core), rep: 2 (over x).
Axes of the slice: x: 2, y: 2, z: 4, core: 2. Of those that a mesh axis runs over, the one named last changes fastest.
Arguments:
- embeddings: bfloat16 [11264, 1024], P(('rows', 'rep')), may hold values from -6 to 6
- owner_ids: int32 [11264, 1], P(('rows', 'rep')), may hold values from 0 to 15; in each aligned block of 352 rows (0 to 351, 352 to 703, ...) at most 64 rows name the same one
- live_mask: int32 [11264], P(('rows', 'rep')), may hold values 0 or 1
Outputs:
- neighbour_means: bfloat16 [11264, 1024], P(('rows', 'rep'))
Inputs may be any that keep to these rules, and one draw needn't show every extreme that they name: `owner_ids`: among the rows of one device, at most 64 name the same owner, and in every draw some owner is named by exactly 64 of them.
All inputs are finite; a program needn't handle non-finite values. Where the computation divides by a largest or mean magnitude, that divisor is 1e-20 or more. No bound on the sum of `live_mask` on one device may be relied on, other than what follows from the above.
Results may differ from a plain program's by a relative error of at most 0.0017.
The roundings to bfloat16 on the way count: a program that leaves them out, or rounds other values in their place, can miss the bound.
Values may be sent and summed in bfloat16 or wider, within the bound.
A program may use at most 64 MiB of HBM per device.

v0:
```python
import jax
import jax.numpy as jnp
from jax import lax
from jax.sharding import PartitionSpec as P

BUCKET = 1024


KERNEL_SCALE = 4.0
EPSILON = 1e-06
PRECISE = lax.Precision.HIGHEST


def block_positions(owner_block, owners, slot_cap):
    onehot = (owner_block[:, None] == jnp.arange(owners, dtype=jnp.int32)[None, :]).astype(
        jnp.int32
    )
    before = jnp.cumsum(onehot, axis=0) - onehot
    slot_rank = jnp.sum(before * onehot, axis=1)
    return owner_block * slot_cap + slot_rank


def whiten(embedded, inverse_root):
    mapped = jnp.dot(embedded, inverse_root, preferred_element_type=jnp.float32)
    return (mapped * lax.rsqrt(jnp.mean(mapped * mapped, axis=1, keepdims=True) + EPSILON)).astype(
        jnp.bfloat16
    )


def bucket_means(members, alive):
    scores = jnp.dot(members, members.T, preferred_element_type=jnp.float32)
    weights = jnp.exp(KERNEL_SCALE * (scores / members.shape[1] - 1.0)) * alive[None, :]
    denominator = jnp.sum(weights, axis=1, keepdims=True)
    summed = jnp.dot(weights.astype(jnp.bfloat16), members, preferred_element_type=jnp.float32)
    averaged = summed / jnp.where(alive[:, None] > 0, denominator, 1.0)
    normed = averaged * lax.rsqrt(jnp.mean(averaged * averaged, axis=1, keepdims=True) + EPSILON)
    return (normed * alive[:, None]).astype(jnp.bfloat16)


def spread(values, positions, slots_all):
    return jnp.zeros((slots_all,) + values.shape[1:], values.dtype).at[positions].set(values)


def first_rows(start_y, first_row, row_share):
    y_rows = lax.dynamic_slice_in_dim(start_y, first_row, row_share, 0)
    return 0.5 * (3.0 * y_rows - jnp.dot(y_rows, start_y, precision=PRECISE))


def second_rows(next_y, next_z, first_row, row_share):
    z_rows = lax.dynamic_slice_in_dim(next_z, first_row, row_share, 0)
    product = jnp.dot(z_rows, next_y, precision=PRECISE)
    return 0.5 * (3.0 * z_rows - jnp.dot(product, next_z, precision=PRECISE))


def per_device(embeddings, owner_ids, live_mask):
    rows_here, columns = embeddings.shape
    owners = lax.axis_size("rows")
    slot_cap = BUCKET // owners
    positions = block_positions(owner_ids[:, 0], owners, slot_cap)
    live_rows = live_mask.astype(jnp.bfloat16)
    masked = embeddings * live_rows[:, None]
    partial_moment = lax.dot_general(
        masked, masked, (((0,), (0,)), ((), ())), preferred_element_type=jnp.float32
    )
    moment = lax.psum(partial_moment, ("rows", "rep"))
    start_y = moment / jnp.max(jnp.sum(jnp.abs(moment), axis=1))
    next_z = 0.5 * (3.0 * jnp.eye(columns, dtype=jnp.float32) - start_y)
    row_share = columns // lax.axis_size("rep")
    first_row = lax.axis_index("rep") * row_share
    next_y = lax.all_gather(first_rows(start_y, first_row, row_share), "rep", axis=0, tiled=True)
    inverse_root = lax.all_gather(
        second_rows(next_y, next_z, first_row, row_share).astype(jnp.bfloat16),
        "rep",
        axis=0,
        tiled=True,
    )
    whitened = whiten(embeddings, inverse_root)
    sent_rows, sent_live = (
        lax.all_to_all(
            spread(whitened, positions, BUCKET).reshape(owners, slot_cap, columns),
            "rows",
            split_axis=0,
            concat_axis=0,
            tiled=True,
        ),
        lax.all_to_all(
            spread(live_rows, positions, BUCKET).reshape(owners, slot_cap),
            "rows",
            split_axis=0,
            concat_axis=0,
            tiled=True,
        ),
    )
    members = sent_rows.reshape(BUCKET, columns)
    member_live = sent_live.reshape(BUCKET).astype(jnp.float32)
    means = bucket_means(members, member_live)
    returned = lax.all_to_all(
        means.reshape(owners, slot_cap, columns), "rows", split_axis=0, concat_axis=0, tiled=True
    )
    return returned.reshape(BUCKET, columns)[positions]


def solution(mesh):
    placed = (P(("rows", "rep"), None), P(("rows", "rep"), None), P(("rows", "rep")))
    return jax.shard_map(
        per_device, mesh=mesh, in_specs=placed, out_specs=P(("rows", "rep"), None), check_vma=False
    )
```

profile of v0, /device:TPU:0, one launch (start us, length us, event | category | flops | bytes accessed | tf_op | source)
XLA Modules:
  0.0 403.8 jit_solution(2860625432853445525)
XLA Ops:
  6.5 0.0 all-reduce.3.cloned.1.call-start
  6.5 0.7 convert_element_type.41
  7.2 4.6 %fusion.21 = f32[1024,1024]{1,0:T(8,128)} fusion(bf16[352,1024]{1,0:T(8,128)(2,1)} %param.3, bf16[352]{0:T(512)(128)(2,1)S(1)} %convert_element_type.41), kind=kOutput, calls=%fused_computation.30 | convolution fusion | flops 738557952 | bytes 4915904 | tf_op jit(solution)/shard_map/dot_general | solution.py:62
  11.9 0.0 all-reduce.3.cloned.1.call-update
  11.9 0.0 all-gather.3.cloned.1.call-start
  11.9 145.5 %all-reduce.3.cloned.1.call-done = f32[1024,1024]{1,0:T(8,128)} async-done(((f32[1024,1024]{1,0:T(8,128)}), f32[1024,1024]{1,0:T(8,128)}) %all-reduce.3.cloned.1.call-update) | async-done | bytes 4194320 | tf_op jit(solution)/shard_map/psum | solution.py:65
  157.5 2.6 abs_reduce_fusion
  160.0 0.6 reduce_max.9
  160.6 5.7 %subtract_multiply_fusion = (f32[1024,1024]{1,0:T(8,128)}, f32[1024,1024]{1,0:T(8,128)S(1)}) fusion(f32[1024,1024]{1,0:T(8,128)} %all-reduce.3.cloned.1.call-done, f32[]{:T(128)} %reduce_max.9), kind=kLoop, calls=%fused_computation.6 | loop fusion | flops 5242880 | bytes 12582916 | tf_op jit(solution)/shard_map/mul | solution.py:67
  166.4 8.4 %subtract_multiply_fusion.1 = f32[512,1024]{1,0:T(8,128)} fusion(f32[1024,1024]{1,0:T(8,128)S(1)} %get-tuple-element.6, s32[]{:T(128)S(6)} %select_n.20), kind=kOutput, calls=%fused_computation.18 | convolution fusion | flops 6444023808 | bytes 10486784 | tf_op jit(solution)/shard_map/dot_general | solution.py:46
  174.8 0.0 all-gather.3.cloned.1.call-update
  174.8 0.2 all-gather.5.cloned.1.call-start
  175.0 55.6 %all-gather.3.cloned.1.call-done = f32[1024,1024]{1,0:T(8,128)} async-done(((f32[512,1024]{1,0:T(8,128)}), f32[1024,1024]{1,0:T(8,128)}) %all-gather.3.cloned.1.call-update) | async-done | bytes 4194320 | tf_op jit(solution)/shard_map/all_gather | solution.py:70
  230.6 0.0 copy-start
  230.6 10.0 %fusion.10 = f32[512,1024]{1,0:T(8,128)S(1)} fusion(f32[1024,1024]{1,0:T(8,128)} %all-gather.3.cloned.1.call-done, f32[1024,1024]{1,0:T(8,128)} %get-tuple-element.5, s32[]{:T(128)S(6)} %select_n.20), kind=kOutput, calls=%fused_computation.22 | convolution fusion | flops 6442450944 | bytes 8388612 | tf_op jit(solution)/shard_map/dot_general | solution.py:51
  240.6 0.0 copy-done
  240.6 0.0 copy-start.2
  240.6 0.0 copy-start.1
  240.7 8.0 %multiply_convert_fusion.1 = bf16[512,1024]{1,0:T(8,128)(2,1)} fusion(f32[1024,1024]{1,0:T(8,128)S(1)} %copy-done, s32[]{:T(128)S(6)} %select_n.20, f32[512,1024]{1,0:T(8,128)S(1)} %fusion.10), kind=kOutput, calls=%fused_computation.17 | convolution fusion | flops 6444548096 | bytes 9437188 | tf_op jit(solution)/shard_map/dot_general | solution.py:52
  248.7 0.0 all-gather.5.cloned.1.call-update
  248.7 0.0 copy-done.2
  248.8 0.9 reduce-window.6
  249.6 0.2 slice_reduce_fusion
  249.9 0.1 bitcast_bitcast_fusion
  250.0 2.8 scatter_custom_fusion.1
  252.8 0.7 all_to_all.16
  253.5 5.6 %all-to-all-start.1 = ((bf16[16,1,64]{2,1,0:T(2,128)(2,1)}), bf16[16,1,64]{2,1,0:T(2,128)(2,1)S(1)}, u32[]{:S(2)}, u32[]{:S(2)}) async-start(bf16[16,1,64]{2,1,0:T(2,128)(2,1)} %all_to_all.16), calls=%async_computation.1 | async-start | bytes 16384 | tf_op jit(solution)/shard_map/all_to_all | solution.py:86
  259.1 22.9 %all-gather.5.cloned.1.call-done = bf16[1024,1024]{1,0:T(8,128)(2,1)} async-done(((bf16[512,1024]{1,0:T(8,128)(2,1)}), bf16[1024,1024]{1,0:T(8,128)(2,1)}) %all-gather.5.cloned.1.call-update) | async-done | bytes 2097168 | tf_op jit(solution)/shard_map/all_gather | solution.py:71
  282.0 0.0 copy-done.1
  282.0 2.6 multiply_reduce_fusion.1
  284.6 3.7 scatter_custom_fusion
  288.3 0.0 all-to-all-done.1
  288.3 5.6 %all-to-all-start = ((bf16[16,64,1024]{2,1,0:T(8,128)(2,1)}), bf16[16,64,1024]{2,1,0:T(8,128)(2,1)S(1)}, u32[]{:S(2)}, u32[]{:S(2)}) async-start(bf16[16,64,1024]{2,1,0:T(8,128)(2,1)} %bitcast.2), calls=%async_computation | async-start | bytes 4194304 | tf_op jit(solution)/shard_map/all_to_all | solution.py:79
  293.9 0.1 reshape.77
  294.0 41.0 %all-to-all-done = bf16[16,64,1024]{2,1,0:T(8,128)(2,1)S(1)} async-done(((bf16[16,64,1024]{2,1,0:T(8,128)(2,1)}), bf16[16,64,1024]{2,1,0:T(8,128)(2,1)S(1)}, u32[]{:S(2)}, u32[]{:S(2)}) %all-to-all-start) | async-done | bytes 2097184 | tf_op jit(solution)/shard_map/all_to_all | solution.py:79
  335.0 2.7 fusion
  337.8 2.7 multiply_reduce_fusion
  340.5 1.8 multiply_convert_fusion
  342.3 11.2 %all-to-all-start.2 = ((bf16[16,64,1024]{2,1,0:T(8,128)(2,1)}), bf16[16,64,1024]{2,1,0:T(8,128)(2,1)S(1)}, u32[]{:S(2)}, u32[]{:S(2)}) async-start(bf16[16,64,1024]{2,1,0:T(8,128)(2,1)} %bitcast.30), calls=%async_computation.2 | async-start | bytes 4194304 | tf_op jit(solution)/shard_map/all_to_all | solution.py:97
  353.5 41.1 %all-to-all-done.2 = bf16[16,64,1024]{2,1,0:T(8,128)(2,1)S(1)} async-done(((bf16[16,64,1024]{2,1,0:T(8,128)(2,1)}), bf16[16,64,1024]{2,1,0:T(8,128)(2,1)S(1)}, u32[]{:S(2)}, u32[]{:S(2)}) %all-to-all-start.2) | async-done | bytes 2097184 | tf_op jit(solution)/shard_map/all_to_all | solution.py:97
  394.6 2.7 gather_fusion
  (11 shorter events, 0.2 us)
Async XLA Ops:
  6.5 150.9 %all-reduce.3.cloned.1.call-start = ((), (), s32[]{:S(2)}) async-start(), calls=%async_computation.3 | async-start | bytes 8388608 | tf_op jit(solution)/shard_map/psum | solution.py:65
  11.9 218.7 %all-gather.3.cloned.1.call-start = ((), (), s32[]{:S(2)}) async-start(), calls=%async_computation.4 | async-start | bytes 6291456 | tf_op jit(solution)/shard_map/all_gather | solution.py:70
  174.8 107.2 %all-gather.5.cloned.1.call-start = ((), (), s32[]{:S(2)}) async-start(), calls=%async_computation.5 | async-start | bytes 3145728 | tf_op jit(solution)/shard_map/all_gather | solution.py:71
  230.6 10.0 %copy-start = (f32[1024,1024]{1,0:T(8,128)S(1)}, f32[1024,1024]{1,0:T(8,128)}, u32[]{:S(2)}) copy-start(f32[1024,1024]{1,0:T(8,128)} %get-tuple-element.5) | copy-start | bytes 12582916
  240.6 8.1 %copy-start.2 = (s32[352,1]{0,1:T(1,128)S(1)}, s32[352,1]{0,1:T(1,128)}, u32[]{:S(2)}) copy-start(s32[352,1]{0,1:T(1,128)} %param.4) | copy-start | bytes 4228
  240.6 41.3 %copy-start.1 = (bf16[352,1024]{1,0:T(8,128)(2,1)S(1)}, bf16[352,1024]{1,0:T(8,128)(2,1)}, u32[]{:S(2)}) copy-start(bf16[352,1024]{1,0:T(8,128)(2,1)} %param.3) | copy-start | bytes 2162692
  253.5 34.8 %all-to-all-start.1 = ((bf16[16,1,64]{2,1,0:T(2,128)(2,1)}), bf16[16,1,64]{2,1,0:T(2,128)(2,1)S(1)}, u32[]{:S(2)}, u32[]{:S(2)}) async-start(bf16[16,1,64]{2,1,0:T(2,128)(2,1)} %all_to_all.16), calls=%async_computation.1 | async-start | bytes 16384 | tf_op jit(solution)/shard_map/all_to_all | solution.py:86
  288.3 46.7 %all-to-all-start = ((bf16[16,64,1024]{2,1,0:T(8,128)(2,1)}), bf16[16,64,1024]{2,1,0:T(8,128)(2,1)S(1)}, u32[]{:S(2)}, u32[]{:S(2)}) async-start(bf16[16,64,1024]{2,1,0:T(8,128)(2,1)} %bitcast.2), calls=%async_computation | async-start | bytes 4194304 | tf_op jit(solution)/shard_map/all_to_all | solution.py:79
  342.3 52.3 %all-to-all-start.2 = ((bf16[16,64,1024]{2,1,0:T(8,128)(2,1)}), bf16[16,64,1024]{2,1,0:T(8,128)(2,1)S(1)}, u32[]{:S(2)}, u32[]{:S(2)}) async-start(bf16[16,64,1024]{2,1,0:T(8,128)(2,1)} %bitcast.30), calls=%async_computation.2 | async-start | bytes 4194304 | tf_op jit(solution)/shard_map/all_to_all | solution.py:97
Sparse Core Ops, SparseCore 0:
  12.9 144.5 all-reduce.2
  174.9 55.6 all-gather.2
  248.8 33.1 all-gather.4
where the time goes:
time: 410 us; the launch traced here: 404 us
  waiting for transfers between devices  306 us (75%)
  matrix products  39.1 us (10%)
  starting transfers between devices  22.7 us (6%)
  other arithmetic  16.2 us (4%)
  between operations  13.2 us (3%)
  local copies, waits for them, and re-layouts  6.39 us (2%)
    psum x1, waiting for transfers between devices, per_device(): moment = lax.psum(partial_moment, ('rows', 'rep'))  146 us
    all_gather x1, waiting for transfers between devices, per_device(): lax.all_gather(first_rows(start_y, first_row, row_share), 'rep', axis=0,...  55.6 us
    all_to_all x1, waiting for transfers between devices, per_device(): lax.all_to_all(means.reshape(owners, slot_cap, columns), 'rows', split_ax...  41.1 us
    all_to_all x1, waiting for transfers between devices, per_device(): lax.all_to_all(spread(whitened, positions, BUCKET).reshape(owners, slot_c...  41 us
    all_gather x1, waiting for transfers between devices, per_device(): lax.all_gather(second_rows(next_y, next_z, first_row, row_share).astype(j...  22.9 us
    all_to_all x1, starting transfers between devices, per_device(): lax.all_to_all(means.reshape(owners, slot_cap, columns), 'rows', split_ax...  11.2 us
    dot_general x1, matrix products, second_rows(): product = jnp.dot(z_rows, next_y, precision=PRECISE)  10 us
    dot_general x1, matrix products, first_rows(): return 0.5 * (3.0 * y_rows - jnp.dot(y_rows, start_y, precision=PRECISE))  8.4 us
  transfers between devices with their start and end apart: 6, of which 5 were waited for; matrix products, arithmetic and copies ran while one was open for 3% of the time, Pallas kernels for 0%

commit v1 on v0

v1 whole, which is shorter than its diff:
```python
import jax
import jax.numpy as jnp
from jax import lax
from jax.sharding import PartitionSpec as P

BUCKET = 1024
JOIN_ROWS = 8192
KERNEL_SCALE = 4.0
EPSILON = 1e-06
SPLIT = lax.Precision.HIGH
PRECISE = lax.Precision.HIGHEST


def block_positions(owner_block, owners, slot_cap):
    rows = owner_block.shape[0]
    same = owner_block[:, None] == owner_block[None, :]
    index = jnp.arange(rows, dtype=jnp.int32)
    earlier = index[None, :] < index[:, None]
    slot_rank = jnp.sum((same & earlier).astype(jnp.int32), axis=1)
    return owner_block * slot_cap + slot_rank


def whiten(embedded, inverse_root):
    mapped = jnp.dot(embedded, inverse_root, preferred_element_type=jnp.float32)
    return (mapped * lax.rsqrt(jnp.mean(mapped * mapped, axis=1, keepdims=True) + EPSILON)).astype(
        jnp.bfloat16
    )


def root_of(moment):
    y = moment / jnp.max(jnp.sum(jnp.abs(moment), axis=1))
    eye = jnp.eye(y.shape[0], dtype=jnp.float32)
    square = jnp.dot(y, y, precision=SPLIT)
    inner = 1.6875 * eye - 0.5625 * y + 0.0625 * square
    return (2.25 * eye - 2.4375 * y + jnp.dot(square, inner, precision=SPLIT)).astype(jnp.bfloat16)


def masked_means(queries, members, same, alive):
    scores = lax.dot_general(
        queries, members, (((1,), (1,)), ((), ())), preferred_element_type=jnp.float32
    )
    weights = jnp.where(same, jnp.exp(KERNEL_SCALE * (scores / members.shape[1] - 1.0)), 0.0)
    denominator = jnp.sum(weights, axis=1, keepdims=True)
    summed = jnp.dot(weights.astype(jnp.bfloat16), members, preferred_element_type=jnp.float32)
    averaged = summed / jnp.where(alive[:, None] > 0, denominator, 1.0)
    normed = averaged * lax.rsqrt(jnp.mean(averaged * averaged, axis=1, keepdims=True) + EPSILON)
    return (normed * alive[:, None]).astype(jnp.bfloat16)


def spread(values, positions, slots_all):
    return jnp.zeros((slots_all,) + values.shape[1:], values.dtype).at[positions].set(values)


def by_exchange(embeddings, owner_ids, live_mask):
    rows_here, columns = embeddings.shape
    owners = lax.axis_size("rows")
    slot_cap = BUCKET // owners
    positions = block_positions(owner_ids[:, 0], owners, slot_cap)
    live_rows = live_mask.astype(jnp.bfloat16)
    masked = embeddings * live_rows[:, None]
    partial_moment = lax.dot_general(
        masked, masked, (((0,), (0,)), ((), ())), preferred_element_type=jnp.float32
    )
    inverse_root = root_of(lax.psum(partial_moment, ("rows", "rep")))
    whitened = whiten(embeddings, inverse_root)

    def swapped(values):
        return lax.all_to_all(values, "rows", split_axis=0, concat_axis=0, tiled=True)

    members = swapped(
        spread(whitened, positions, BUCKET).reshape(owners, slot_cap, columns)
    ).reshape(BUCKET, columns)
    alive = swapped(spread(live_rows, positions, BUCKET).reshape(owners, slot_cap))
    alive = alive.reshape(BUCKET).astype(jnp.float32)
    means = masked_means(members, members, alive[None, :] > 0, alive)
    returned = swapped(means.reshape(owners, slot_cap, columns))
    return returned.reshape(BUCKET, columns)[positions]


def by_gather(embeddings, owner_ids, live_mask):
    rows_here, columns = embeddings.shape
    owners = lax.axis_size("rows")
    key = jnp.where(live_mask > 0, owner_ids[:, 0], -1)
    keys = lax.all_gather(key, "rows", axis=0, tiled=True)
    everyone = lax.all_gather(embeddings, "rows", axis=0, tiled=True)
    share = columns // owners
    masked = everyone * (keys >= 0).astype(jnp.bfloat16)[:, None]
    own = lax.dynamic_slice_in_dim(masked, lax.axis_index("rows") * share, share, 1)
    part = lax.dot_general(own, masked, (((0,), (0,)), ((), ())), preferred_element_type=jnp.float32)
    part = lax.psum(part, "rep")
    moment = lax.all_gather(part, "rows", axis=0, tiled=True)
    whitened = whiten(everyone, root_of(moment))
    mine = lax.dynamic_slice_in_dim(whitened, lax.axis_index("rows") * rows_here, rows_here, 0)
    alive = (live_mask > 0).astype(jnp.float32)
    return masked_means(mine, whitened, owner_ids == keys[None, :], alive)


def solution(mesh):
    placed = (P(("rows", "rep"), None), P(("rows", "rep"), None), P(("rows", "rep")))

    def per_device(embeddings, owner_ids, live_mask):
        gathered = embeddings.shape[0] * mesh.shape["rows"]
        join = by_gather if gathered <= JOIN_ROWS else by_exchange
        return join(embeddings, owner_ids, live_mask)

    return jax.shard_map(
        per_device, mesh=mesh, in_specs=placed, out_specs=P(("rows", "rep"), None), check_vma=False
    )
```

time: 410 us -> 266 us (0.65); the launches traced: 404 us -> 266 us
  waiting for transfers between devices: 306 us -> 107 us
  blocking collectives: 0 us -> 65.3 us
  starting transfers between devices: 22.7 us -> 0.08 us
  matrix products: 39.1 us -> 57.3 us
  other arithmetic: 16.2 us -> 21.4 us
  local copies, waits for them, and re-layouts: 6.39 us -> 1.25 us
    psum x1, waiting for transfers between devices: 146 us -> 21.7 us  [by_gather(): part = lax.psum(part, 'rep')]
    all_to_all x3 -> x0, waiting for transfers between devices: 82.1 us -> none  [the longest x1 41.1 us: per_device(): lax.all_to_all(means.reshape(owners, slot_cap, columns), 'rows', split_ax...]
    unnamed x0 -> x1, blocking collectives: none -> 65.3 us
    all_to_all x3 -> x0, starting transfers between devices: 22.5 us -> none  [the longest x1 11.2 us: per_device(): lax.all_to_all(means.reshape(owners, slot_cap, columns), 'rows', split_ax...]
    dot_general x1, matrix products: 2.59 us -> 19.5 us  [whiten(): mapped = jnp.dot(embedded, inverse_root, preferred_element_type=jnp.float32)]
    convert_element_type x3 -> x4, other arithmetic: 2.51 us -> 10.4 us  [the longest x1 8.69 us: whiten(): (mapped * lax.rsqrt(jnp.mean(mapped * mapped, axis=1, keepdims=True) + EP...]
    all_gather x2, waiting for transfers between devices: 78.4 us -> 84.2 us  [the longest x1 53 us: by_gather(): moment = lax.all_gather(part, 'rows', axis=0, tiled=True)]
    dot_general x6 -> x5, matrix products: 36.5 us -> 37.8 us  [the longest x1 11.7 us: root_of(): square = jnp.dot(y, y, precision=SPLIT)]
  transfers between devices with their start and end apart: 6 -> 3, of which waited for: 5 -> 3; matrix products, arithmetic and copies ran while one was open for 3% -> 1% of each run, Pallas kernels for 0% -> 0%
where the time goes in v1:
time: 266 us
  waiting for transfers between devices  107 us (40%)
  blocking collectives  65.3 us (25%)
  matrix products  57.3 us (22%)
  other arithmetic  21.4 us (8%)
  between operations  13.8 us (5%)
    unnamed x1, blocking collectives  65.3 us
    all_gather x1, waiting for transfers between devices, by_gather(): moment = lax.all_gather(part, 'rows', axis=0, tiled=True)  53 us
    all_gather x1, waiting for transfers between devices, by_gather(): everyone = lax.all_gather(embeddings, 'rows', axis=0, tiled=True)  31.2 us
    psum x1, waiting for transfers between devices, by_gather(): part = lax.psum(part, 'rep')  21.7 us
    dot_general x1, matrix products, whiten(): mapped = jnp.dot(embedded, inverse_root, preferred_element_type=jnp.float32)  19.5 us
    dot_general x1, matrix products, root_of(): square = jnp.dot(y, y, precision=SPLIT)  11.7 us
    convert_element_type x1, other arithmetic, whiten(): (mapped * lax.rsqrt(jnp.mean(mapped * mapped, axis=1, keepdims=True) + EP...  8.69 us
    dot_general x1, matrix products, root_of(): jnp.dot(square, inner, precision=SPLIT)  8.6 us
  transfers between devices with their start and end apart: 3, of which 3 were waited for; matrix products, arithmetic and copies ran while one was open for 1% of the time, Pallas kernels for 0%

profile of v1, /device:TPU:0, one launch (start us, length us, event | category | flops | bytes accessed | tf_op | source)
XLA Modules:
  0.0 265.8 jit_solution(3059865663002023440)
XLA Ops:
  6.5 0.0 all-gather.3.cloned.1.call-start
  6.5 0.7 all-gather.3.cloned.1.call-update
  7.3 0.0 all-reduce.3.cloned.1.call-start
  7.3 0.7 reduce.1
  8.0 1.2 dynamic-slice.4
  9.9 0.7 fusion.31
  10.6 0.1 select_dynamic-update-slice_fusion
  10.7 65.3 %all-reduce = s32[5632]{0:T(1024)S(1)} all-reduce(s32[5632]{0:T(1024)S(1)} %select_dynamic-update-slice_fusion), channel_id=1, replica_groups=mesh['rows'=16,'rep'=2] {'rows'}, use_global_device_ids=true, to_apply=%add | all-reduce | flops 5632 | bytes 45056
  76.0 31.2 %all-gather.3.cloned.1.call-done = bf16[5632,1024]{1,0:T(8,128)(2,1)} async-done(((bf16[352,1024]{1,0:T(8,128)(2,1)}), bf16[5632,1024]{1,0:T(8,128)(2,1)}) %all-gather.3.cloned.1.call-update) | async-done | bytes 11534352 | tf_op jit(solution)/shard_map/all_gather | solution.py:85
  107.2 7.0 %broadcast_multiply_fusion = bf16[5632,1024]{1,0:T(8,128)(2,1)S(1)} fusion(bf16[5632,1024]{1,0:T(8,128)(2,1)} %all-gather.3.cloned.1.call-done, bf16[5632]{0:T(1024)(128)(2,1)S(1)} %compare_convert_fusion), kind=kLoop, calls=%fused_computation.7 | loop fusion | flops 5767168 | bytes 23079936 | tf_op jit(solution)/shard_map/mul | solution.py:87
  114.2 3.3 %fusion.19 = f32[64,1024]{1,0:T(8,128)} fusion(bf16[5632,1024]{1,0:T(8,128)(2,1)S(1)} %broadcast_multiply_fusion, s32[]{:T(128)S(6)} %select_n.20), kind=kOutput, calls=%fused_computation.27 | convolution fusion | flops 738197504 | bytes 13238276 | tf_op jit(solution)/shard_map/dot_general | solution.py:89
  117.5 0.0 all-reduce.3.cloned.1.call-update
  117.5 0.0 all-gather.5.cloned.1.call-start
  117.6 21.7 %all-reduce.3.cloned.1.call-done = f32[64,1024]{1,0:T(8,128)} async-done(((f32[64,1024]{1,0:T(8,128)}), f32[64,1024]{1,0:T(8,128)}) %all-reduce.3.cloned.1.call-update) | async-done | bytes 262160 | tf_op jit(solution)/shard_map/psum | solution.py:90
  139.3 0.0 all-gather.5.cloned.1.call-update
  139.3 53.0 %all-gather.5.cloned.1.call-done = f32[1024,1024]{1,0:T(8,128)} async-done(((f32[64,1024]{1,0:T(8,128)}), f32[1024,1024]{1,0:T(8,128)}) %all-gather.5.cloned.1.call-update) | async-done | bytes 4194320 | tf_op jit(solution)/shard_map/all_gather | solution.py:91
  192.3 2.6 abs_reduce_fusion
  194.8 0.6 reduce_max.9
  195.4 0.0 copy-start
  195.4 11.7 %fusion.18 = f32[1024,1024]{1,0:T(8,128)S(1)} fusion(f32[1024,1024]{1,0:T(8,128)} %all-gather.5.cloned.1.call-done, f32[]{:T(128)} %reduce_max.9), kind=kOutput, calls=%fused_computation.24 | convolution fusion | flops 6443499520 | bytes 8388612 | tf_op jit(solution)/shard_map/dot_general | solution.py:33
  207.2 0.0 copy-done
  207.2 8.6 %add_convert_fusion = bf16[1024,1024]{1,0:T(8,128)(2,1)S(1)} fusion(f32[1024,1024]{1,0:T(8,128)S(1)} %fusion.18, f32[1024,1024]{1,0:T(8,128)S(1)} %copy-done, f32[]{:T(128)} %reduce_max.9), kind=kOutput, calls=%fused_computation.8 | convolution fusion | flops 6457131008 | bytes 10485764 | tf_op jit(solution)/shard_map/dot_general | solution.py:35
  215.8 19.5 %multiply_reduce_fusion = (f32[5632]{0:T(1024)S(1)}, f32[1024,5632]{1,0:T(8,128)}) fusion(bf16[1024,1024]{1,0:T(8,128)(2,1)S(1)} %add_convert_fusion, bf16[5632,1024]{1,0:T(8,128)(2,1)} %all-gather.3.cloned.1.call-done), kind=kOutput, calls=%fused_computation.1 | convolution fusion | flops 11822688256 | bytes 36722688 | tf_op jit(solution)/shard_map/dot_general | solution.py:24
  235.3 8.7 %multiply_convert_fusion = bf16[1024,5632]{1,0:T(8,128)(2,1)S(1)} fusion(f32[1024,5632]{1,0:T(8,128)} %get-tuple-element.8, f32[5632]{0:T(1024)S(1)} %add_rsqrt_fusion), kind=kLoop, calls=%fused_computation | loop fusion | flops 11534336 | bytes 34625536 | tf_op jit(solution)/shard_map/convert_element_type | solution.py:25
  244.0 7.7 %fusion.32 = (f32[352]{0:T(512)S(1)}, bf16[352,5632]{1,0:T(8,128)(2,1)}) fusion(bf16[1024,5632]{1,0:T(8,128)(2,1)S(1)} %multiply_convert_fusion, s32[]{:T(128)S(6)} %select_n.21, s32[5632]{0:T(1024)S(1)} %all-reduce, s32[352]{0:T(512)S(1)} %reduce.1), kind=kOutput, calls=%fused_computation.44 | convolution fusion | flops 4073963264 | bytes 16313732 | tf_op jit(solution)/shard_map/dot_general | solution.py:39
  251.7 6.5 %multiply_reduce_fusion.1 = (f32[352]{0:T(512)S(1)}, f32[352,1024]{1,0:T(8,128)S(1)}) fusion(f32[352]{0:T(512)S(1)} %compare_select_fusion, bf16[1024,5632]{1,0:T(8,128)(2,1)S(1)} %multiply_convert_fusion, bf16[352,5632]{1,0:T(8,128)(2,1)} %get-tuple-element.10), kind=kOutput, calls=%fused_computation.26 | convolution fusion | flops 4061167360 | bytes 16943872 | tf_op jit(solution)/shard_map/dot_general | solution.py:44
  258.2 1.1 multiply_convert_fusion.1
  (5 shorter events, 0.0 us)
Async XLA Ops:
  6.5 100.7 %all-gather.3.cloned.1.call-start = ((), (), s32[]{:S(2)}) async-start(), calls=%async_computation | async-start | bytes 12255232 | tf_op jit(solution)/shard_map/all_gather | solution.py:85
  7.3 132.0 %all-reduce.3.cloned.1.call-start = ((), (), s32[]{:S(2)}) async-start(), calls=%async_computation.1 | async-start | bytes 524288 | tf_op jit(solution)/shard_map/psum | solution.py:90
  117.5 74.8 %all-gather.5.cloned.1.call-start = ((), (), s32[]{:S(2)}) async-start(), calls=%async_computation.2 | async-start | bytes 4456448 | tf_op jit(solution)/shard_map/all_gather | solution.py:91
  195.4 11.7 %copy-start = (f32[1024,1024]{1,0:T(8,128)S(1)}, f32[1024,1024]{1,0:T(8,128)}, u32[]{:S(2)}) copy-start(f32[1024,1024]{1,0:T(8,128)} %all-gather.5.cloned.1.call-done) | copy-start | bytes 12582916
Sparse Core Ops, SparseCore 0:
  9.6 97.5 all-gather.2
  117.6 21.6 all-reduce.2
  141.7 50.5 all-gather.4

commit v2 on v1

--- a/solution.py
+++ b/solution.py
@@ -1,6 +1,10 @@
+import functools
+
 import jax
 import jax.numpy as jnp
 from jax import lax
+from jax.experimental import pallas as pl
+from jax.experimental.pallas import tpu as pltpu
 from jax.sharding import PartitionSpec as P
 
 BUCKET = 1024
@@ -77,20 +81,162 @@
     return returned.reshape(BUCKET, columns)[positions]
 
 
+def gather_kernel(owners, reduced, chunks, *refs):
+    if reduced:
+        x_ref, out_ref, other, own, pair_sems, here_sem, z_send, z_recv, y_send, y_recv, c_send, c_recv = refs
+    else:
+        x_ref, out_ref, here_sem, z_send, z_recv, y_send, y_recv, c_send, c_recv = refs
+    me = lax.axis_index("rows")
+    core, y, z = me % 2, (me // 2) % 2, me // 4
+    depth = owners // 4
+
+    def at(z_, y_, core_):
+        return z_ * 4 + y_ * 2 + core_
+
+    beside, sibling = at(z, 1 - y, core), at(z, y, 1 - core)
+    along = [at((z + d) % depth, y, core) for d in range(1, depth)]
+    barrier = pltpu.get_barrier_semaphore()
+    for peer in along + [beside, sibling]:
+        pl.semaphore_signal(
+            barrier, inc=1, device_id={"rows": peer}, device_id_type=pl.DeviceIdType.MESH
+        )
+    if reduced:
+        across = {"rep": 1 - lax.axis_index("rep")}
+        pl.semaphore_signal(
+            barrier, inc=1, device_id=across, device_id_type=pl.DeviceIdType.MESH
+        )
+    pl.semaphore_wait(barrier, depth + 1 + int(reduced))
+
+    source = x_ref
+    if reduced:
+        swap = pltpu.make_async_remote_copy(
+            src_ref=x_ref,
+            dst_ref=other,
+            send_sem=pair_sems.at[0],
+            recv_sem=pair_sems.at[1],
+            device_id=across,
+            device_id_type=pl.DeviceIdType.MESH,
+        )
+        swap.start()
+        swap.wait()
+        own[...] = x_ref[...] + other[...]
+        source = own
+
+    started = []
+
+    def send(block, k, peer, send_sems, recv_sems, n, first=False):
+        rows = pl.ds(*chunks[k])
+        copy = pltpu.make_async_remote_copy(
+            src_ref=source.at[rows] if first else out_ref.at[block, rows],
+            dst_ref=out_ref.at[block, rows],
+            send_sem=send_sems.at[n, k],
+            recv_sem=recv_sems.at[n, k],
+            device_id={"rows": peer},
+            device_id_type=pl.DeviceIdType.MESH,
+        )
+        copy.start()
+        started.append(copy)
+
+    def arrived(block, k, recv_sems, n):
+        rows = pl.ds(*chunks[k])
+        place = out_ref.at[block, rows]
+        pltpu.make_async_copy(place, place, recv_sems.at[n, k]).wait()
+
+    here = pltpu.make_async_copy(source, out_ref.at[me], here_sem)
+    here.start()
+    order = sorted(range(1, depth), key=lambda d: min(d, depth - d))
+    for k in range(len(chunks)):
+        send(me, k, beside, y_send, y_recv, 0, True)
+        for d in order:
+            send(me, k, along[d - 1], z_send, z_recv, d - 1, True)
+        send(me, k, sibling, c_send, c_recv, 0, True)
+    for k in range(len(chunks)):
+        for d in order:
+            block = at((z + depth - d) % depth, y, core)
+            arrived(block, k, z_recv, d - 1)
+            send(block, k, beside, y_send, y_recv, d)
+            send(block, k, sibling, c_send, c_recv, d)
+    for d in [0] + order:
+        for k in range(len(chunks)):
+            block = at((z + depth - d) % depth, 1 - y, core)
+            arrived(block, k, y_recv, d)
+            send(block, k, sibling, c_send, c_recv, depth + d)
+    for d in range(depth):
+        for k in range(len(chunks)):
+            arrived(at((z + depth - d) % depth, y, 1 - core), k, c_recv, d)
+            arrived(at((z + depth - d) % depth, 1 - y, 1 - core), k, c_recv, depth + d)
+    for copy in started:
+        copy.wait_send()
+    here.wait()
+
+
+def plane_gather(block, owners, chunk, collective_id, reduced=False):
+    rows = block.shape[0]
+    chunks = [(start, min(chunk, rows - start)) for start in range(0, rows, chunk)]
+    n, depth = len(chunks), owners // 4
+    dma = pltpu.SemaphoreType.DMA
+    scratch = [dma(())] + [
+        dma((count, n)) for count in (depth - 1, depth - 1, depth, depth, 2 * depth, 2 * depth)
+    ]
+    if reduced:
+        scratch = [
+            pltpu.VMEM(block.shape, block.dtype),
+            pltpu.VMEM(block.shape, block.dtype),
+            dma((2,)),
+        ] + scratch
+    return pl.pallas_call(
+        functools.partial(gather_kernel, owners, reduced, chunks),
+        out_shape=jax.ShapeDtypeStruct((owners,) + block.shape, block.dtype),
+        in_specs=[pl.BlockSpec(memory_space=pltpu.VMEM if reduced else pl.ANY)],
+        out_specs=pl.BlockSpec(memory_space=pl.ANY),
+        scratch_shapes=scratch,
+        compiler_params=pltpu.CompilerParams(
+            collective_id=collective_id, has_side_effects=True, vmem_limit_bytes=16 << 20
+        ),
+    )(block)
+
+
+def whiten_kernel(x_ref, root_ref, out_ref):
+    mapped = jnp.dot(x_ref[...], root_ref[...], preferred_element_type=jnp.float32)
+    scale = lax.rsqrt(jnp.mean(mapped * mapped, axis=1, keepdims=True) + EPSILON)
+    out_ref[...] = (mapped * scale).astype(jnp.bfloat16)
+
+
+def whiten_rows(rows, root, tile):
+    count, columns = rows.shape
+    return pl.pallas_call(
+        whiten_kernel,
+        grid=(count // tile,),
+        out_shape=jax.ShapeDtypeStruct(rows.shape, jnp.bfloat16),
+        in_specs=[
+            pl.BlockSpec((tile, columns), lambda i: (i, 0)),
+            pl.BlockSpec((columns, columns), lambda i: (0, 0)),
+        ],
+        out_specs=pl.BlockSpec((tile, columns), lambda i: (i, 0)),
+        compiler_params=pltpu.CompilerParams(vmem_limit_bytes=32 << 20),
+    )(rows, root)
+
+
 def by_gather(embeddings, owner_ids, live_mask):
     rows_here, columns = embeddings.shape
     owners = lax.axis_size("rows")
     key = jnp.where(live_mask > 0, owner_ids[:, 0], -1)
-    keys = lax.all_gather(key, "rows", axis=0, tiled=True)
-    everyone = lax.all_gather(embeddings, "rows", axis=0, tiled=True)
+    extra = jnp.pad(key.astype(jnp.bfloat16)[None, :], ((0, 15), (0, columns - rows_here)))
+    block = jnp.concatenate([embeddings, extra], axis=0)
+    held = block.shape[0]
+    blocks = plane_gather(block, owners, 96, 1)
+    keys = blocks[:, rows_here, :rows_here].astype(jnp.int32)
+    keys = jnp.pad(keys, ((0, 0), (0, held - rows_here)), constant_values=-1).reshape(-1)
+    everyone = blocks.reshape(owners * held, columns)
     share = columns // owners
-    masked = everyone * (keys >= 0).astype(jnp.bfloat16)[:, None]
-    own = lax.dynamic_slice_in_dim(masked, lax.axis_index("rows") * share, share, 1)
-    part = lax.dot_general(own, masked, (((0,), (0,)), ((), ())), preferred_element_type=jnp.float32)
-    part = lax.psum(part, "rep")
-    moment = lax.all_gather(part, "rows", axis=0, tiled=True)
-    whitened = whiten(everyone, root_of(moment))
-    mine = lax.dynamic_slice_in_dim(whitened, lax.axis_index("rows") * rows_here, rows_here, 0)
+    live = (keys >= 0).astype(jnp.bfloat16)[:, None]
+    own = lax.dynamic_slice_in_dim(everyone, lax.axis_index("rows") * share, share, 1) * live
+    part = lax.dot_general(
+        own, everyone, (((0,), (0,)), ((), ())), preferred_element_type=jnp.float32
+    )
+    moment = plane_gather(part, owners, 32, 2, True).reshape(columns, columns)
+    whitened = whiten_rows(everyone, root_of(moment), held)
+    mine = lax.dynamic_slice_in_dim(whitened, lax.axis_index("rows") * held, rows_here, 0)
     alive = (live_mask > 0).astype(jnp.float32)
     return masked_means(mine, whitened, owner_ids == keys[None, :], alive)
 
@@ -100,7 +246,8 @@
 
     def per_device(embeddings, owner_ids, live_mask):
         gathered = embeddings.shape[0] * mesh.shape["rows"]
-        join = by_gather if gathered <= JOIN_ROWS else by_exchange
+        fits = gathered <= JOIN_ROWS and mesh.shape["rep"] == 2
+        join = by_gather if fits else by_exchange
         return join(embeddings, owner_ids, live_mask)
 
     return jax.shard_map(

time: 266 us -> 212 us (0.80)
  Pallas kernels: 0 us -> 146 us
  waiting for transfers between devices: 107 us -> 0 us
  blocking collectives: 65.3 us -> 0 us
  between operations: 13.8 us -> 0.15 us
  matrix products: 57.3 us -> 45 us
  other arithmetic: 21.4 us -> 9.35 us
  local copies, waits for them, and re-layouts: 1.25 us -> 11 us
    pallas_call x0 -> x3, Pallas kernels: none -> 146 us  [the longest x2 127 us: plane_gather(): pl.pallas_call(functools.partial(gather_kernel, owners, reduced, chunks),...]
    all_gather x2 -> x0, waiting for transfers between devices: 84.2 us -> none  [the longest x1 53 us: by_gather(): moment = lax.all_gather(part, 'rows', axis=0, tiled=True)]
    unnamed x1 -> x0, blocking collectives: 65.3 us -> none
    psum x1 -> x0, waiting for transfers between devices: 21.7 us -> none  [by_gather(): part = lax.psum(part, 'rep')]
    dot_general x2 -> x1, matrix products: 22.8 us -> 8.52 us  [by_gather(): lax.dot_general(own, everyone, (((0,), (0,)), ((), ())), preferred_elemen...]
    unnamed x4 -> x7, local copies, waits for them, and re-layouts: 1.25 us -> 10.9 us
    convert_element_type x2, other arithmetic: 8.69 us -> 0.01 us  [the longest x1 0.01 us: by_gather(): key.astype(jnp.bfloat16)[None, :]]
    dot_general x1, matrix products: 7.72 us -> 12.3 us  [masked_means(): lax.dot_general(queries, members, (((1,), (1,)), ((), ())), preferred_ele...]
  transfers between devices with their start and end apart: 3 -> 0, of which waited for: 3 -> 0; matrix products, arithmetic and copies ran while one was open for 1% -> 0% of each run, Pallas kernels for 0% -> 0%
where the time goes in v2:
time: 212 us
  Pallas kernels  146 us (69%)
  matrix products  45 us (21%)
  local copies, waits for them, and re-layouts  11 us (5%)
  other arithmetic  9.35 us (4%)
    pallas_call x2, Pallas kernels, plane_gather(): pl.pallas_call(functools.partial(gather_kernel, owners, reduced, chunks),...  127 us
    pallas_call x1, Pallas kernels, whiten_rows(): pl.pallas_call(whiten_kernel, grid=(count // tile,), out_shape=jax.ShapeD...  18.7 us
    dot_general x1, matrix products, masked_means(): lax.dot_general(queries, members, (((1,), (1,)), ((), ())), preferred_ele...  12.3 us
    unnamed x7, local copies, waits for them, and re-layouts  10.9 us
    dot_general x1, matrix products, masked_means(): jnp.dot(weights.astype(jnp.bfloat16), members, preferred_element_type=jnp...  8.74 us
    dot_general x1, matrix products, by_gather(): lax.dot_general(own, everyone, (((0,), (0,)), ((), ())), preferred_elemen...  8.52 us
    dot_general x1, matrix products, root_of(): jnp.dot(square, inner, precision=SPLIT)  7.85 us
    dot_general x1, matrix products, root_of(): square = jnp.dot(y, y, precision=SPLIT)  7.52 us

profile of v2, /device:TPU:0, one launch (start us, length us, event | category | flops | bytes accessed | tf_op | source)
XLA Modules:
  0.0 211.5 jit_solution(573487650622586133)
XLA Ops:
  0.0 0.7 fusion.21
  0.7 0.7 reduce.2
  1.4 1.2 fusion.16.refs_0_
  2.6 83.8 %shard_map.37 = bf16[16,368,1024]{2,1,0:T(8,128)(2,1)S(1)} custom-call(bf16[368,1024]{1,0:T(8,128)(2,1)S(1)} %fusion.16.refs_0_), custom_call_target="tpu_custom_call" | custom-call | tf_op jit(solution)/shard_map/pallas_call | solution.py:187
  86.3 0.0 copy-start
  86.4 4.5 %copy-done = bf16[16,368,1024]{2,1,0:T(8,128)(2,1)} copy-done((bf16[16,368,1024]{2,1,0:T(8,128)(2,1)}, bf16[16,368,1024]{2,1,0:T(8,128)(2,1)S(1)}, u32[]{:S(2)}) %copy-start) | copy-done | bytes 12058648
  90.9 0.1 reshape.36
  91.0 8.5 %fusion.9.refs_0_ = f32[64,1024]{1,0:T(8,128)S(1)} fusion(bf16[5888,1024]{1,0:T(8,128)(2,1)} %bitcast.23, s32[]{:T(128)S(6)} %select_n.20, bf16[5888]{0:T(1024)(128)(2,1)S(1)} %compare_convert_fusion), kind=kOutput, calls=%fused_computation.18 | convolution fusion | flops 773259264 | bytes 13839876 | tf_op jit(solution)/shard_map/dot_general | solution.py:234
  99.5 43.6 %shard_map.38 = f32[16,64,1024]{2,1,0:T(8,128)S(1)} custom-call(f32[64,1024]{1,0:T(8,128)S(1)} %fusion.9.refs_0_), custom_call_target="tpu_custom_call" | custom-call | tf_op jit(solution)/shard_map/pallas_call | solution.py:187
  143.1 0.0 copy-start.1
  143.1 2.0 copy-done.1
  145.1 0.4 abs_reduce_fusion
  145.5 0.6 reduce_max.9
  146.1 3.9 %broadcast_multiply_fusion = (f32[16,64,1024]{2,1,0:T(8,128)S(1)}, f32[16,64,1024]{2,1,0:T(8,128)S(1)}) fusion(f32[16,64,1024]{2,1,0:T(8,128)} %copy-done.1, f32[]{:T(128)} %reduce_max.9), kind=kLoop, calls=%fused_computation.14 | loop fusion | flops 2097152 | bytes 12582916 | tf_op jit(solution)/shard_map/mul | solution.py:38
  150.0 7.5 %fusion.4 = (f32[1024,1024]{1,0:T(8,128)S(1)}, f32[1024,1024]{1,0:T(8,128)S(1)}) fusion(f32[16,64,1024]{2,1,0:T(8,128)S(1)} %get-tuple-element.7, f32[1024,1024]{1,0:T(8,128)S(1)} %bitcast.25), kind=kOutput, calls=%fused_computation.6 | convolution fusion | flops 6447693824 | bytes 16777216 | tf_op jit(solution)/shard_map/dot_general | solution.py:37
  157.5 0.8 broadcast_multiply_fusion.1
  158.3 7.8 %fusion.6.root_ref = bf16[1024,1024]{1,0:T(8,128)(2,1)S(1)} fusion(f32[16,64,1024]{2,1,0:T(8,128)S(1)} %broadcast_multiply_fusion.1, f32[1024,1024]{1,0:T(8,128)S(1)} %get-tuple-element.10, f32[1024,1024]{1,0:T(8,128)S(1)} %get-tuple-element.9), kind=kOutput, calls=%fused_computation.9 | convolution fusion | flops 6447693824 | bytes 14680064 | tf_op jit(solution)/shard_map/dot_general | solution.py:39
  166.2 18.7 %shard_map.39 = bf16[5888,1024]{1,0:T(8,128)(2,1)S(1)} custom-call(bf16[5888,1024]{1,0:T(8,128)(2,1)} %bitcast.24, bf16[1024,1024]{1,0:T(8,128)(2,1)S(1)} %fusion.6.root_ref), custom_call_target="tpu_custom_call" | custom-call | tf_op jit(solution)/shard_map/pallas_call | solution.py:207
  184.9 0.0 copy-start.2
  184.9 4.5 %copy-done.2 = bf16[5888,1024]{1,0:T(8,128)(2,1)} copy-done((bf16[5888,1024]{1,0:T(8,128)(2,1)}, bf16[5888,1024]{1,0:T(8,128)(2,1)S(1)}, u32[]{:S(2)}) %copy-start.2) | copy-done | bytes 12058648
  189.4 12.3 %fusion.22 = (f32[352]{0:T(512)S(1)}, bf16[352,5888]{1,0:T(8,128)(2,1)}) fusion(bf16[5888,1024]{1,0:T(8,128)(2,1)} %copy-done.2, s32[]{:T(128)S(6)} %select_n.21, s32[5888]{0:T(1024)S(1)} %reshape.36, s32[352]{0:T(512)S(1)} %reduce.2), kind=kOutput, calls=%fused_computation.38 | convolution fusion | flops 4259143424 | bytes 16951044 | tf_op jit(solution)/shard_map/dot_general | solution.py:43
  201.7 8.7 %multiply_reduce_fusion = (f32[352]{0:T(512)S(1)}, f32[352,1024]{1,0:T(8,128)S(1)}) fusion(f32[352]{0:T(512)S(1)} %compare_select_fusion, bf16[5888,1024]{1,0:T(8,128)(2,1)} %copy-done.2, bf16[352,5888]{1,0:T(8,128)(2,1)} %get-tuple-element.12), kind=kOutput, calls=%fused_computation.23 | convolution fusion | flops 4245716736 | bytes 17648384 | tf_op jit(solution)/shard_map/dot_general | solution.py:48
  210.5 1.1 multiply_convert_fusion
  (8 shorter events, 0.1 us)
Async XLA Ops:
  86.3 4.5 %copy-start = (bf16[16,368,1024]{2,1,0:T(8,128)(2,1)}, bf16[16,368,1024]{2,1,0:T(8,128)(2,1)S(1)}, u32[]{:S(2)}) copy-start(bf16[16,368,1024]{2,1,0:T(8,128)(2,1)S(1)} %shard_map.37) | copy-start | bytes 36175876
  143.1 2.0 copy-start.1
  184.9 4.5 %copy-start.2 = (bf16[5888,1024]{1,0:T(8,128)(2,1)}, bf16[5888,1024]{1,0:T(8,128)(2,1)S(1)}, u32[]{:S(2)}) copy-start(bf16[5888,1024]{1,0:T(8,128)(2,1)S(1)} %shard_map.39) | copy-start | bytes 36175876

commit v3 on v2

--- a/solution.py
+++ b/solution.py
@@ -196,25 +196,67 @@
     )(block)
 
 
-def whiten_kernel(x_ref, root_ref, out_ref):
-    mapped = jnp.dot(x_ref[...], root_ref[...], preferred_element_type=jnp.float32)
+def whitened_block(rows, root):
+    mapped = jnp.dot(rows, root, preferred_element_type=jnp.float32)
     scale = lax.rsqrt(jnp.mean(mapped * mapped, axis=1, keepdims=True) + EPSILON)
-    out_ref[...] = (mapped * scale).astype(jnp.bfloat16)
-
-
-def whiten_rows(rows, root, tile):
-    count, columns = rows.shape
+    return (mapped * scale).astype(jnp.bfloat16)
+
+
+def join_kernel(own_ref, named_ref, alive_ref, root_ref, x_ref, key_ref, out_ref, query, total, norm):
+    step = pl.program_id(0)
+
+    @pl.when(step == 0)
+    def _():
+        query[...] = whitened_block(own_ref[...], root_ref[...])
+        total[...] = jnp.zeros_like(total)
+        norm[...] = jnp.zeros_like(norm)
+
+    members = whitened_block(x_ref[0], root_ref[...])
+    scores = lax.dot_general(
+        query[...], members, (((1,), (1,)), ((), ())), preferred_element_type=jnp.float32
+    )
+    close = jnp.exp(KERNEL_SCALE * (scores * (1.0 / members.shape[1]) - 1.0))
+    weights = jnp.where(named_ref[...] == key_ref[0], close, 0.0)
+    norm[...] += jnp.sum(weights, axis=1, keepdims=True)
+    total[...] += jnp.dot(
+        weights.astype(jnp.bfloat16), members, preferred_element_type=jnp.float32
+    )
+
+    @pl.when(step == pl.num_programs(0) - 1)
+    def _():
+        alive = alive_ref[...]
+        averaged = total[...] / jnp.where(alive > 0, norm[...], 1.0)
+        scale = lax.rsqrt(jnp.mean(averaged * averaged, axis=1, keepdims=True) + EPSILON)
+        out_ref[...] = (averaged * scale * alive).astype(jnp.bfloat16)
+
+
+def join_rows(own, named, alive, root, blocks, keys):
+    rows, columns = own.shape
+    count, held, _ = blocks.shape
+
+    def whole(shape):
+        return pl.BlockSpec(shape, lambda i: (0, 0))
+
     return pl.pallas_call(
-        whiten_kernel,
-        grid=(count // tile,),
-        out_shape=jax.ShapeDtypeStruct(rows.shape, jnp.bfloat16),
+        join_kernel,
+        grid=(count,),
+        out_shape=jax.ShapeDtypeStruct(own.shape, jnp.bfloat16),
         in_specs=[
-            pl.BlockSpec((tile, columns), lambda i: (i, 0)),
-            pl.BlockSpec((columns, columns), lambda i: (0, 0)),
+            whole(own.shape),
+            whole(named.shape),
+            whole(alive.shape),
+            whole(root.shape),
+            pl.BlockSpec((1, held, columns), lambda i: (i, 0, 0)),
+            pl.BlockSpec((1, 1, held), lambda i: (i, 0, 0)),
         ],
-        out_specs=pl.BlockSpec((tile, columns), lambda i: (i, 0)),
-        compiler_params=pltpu.CompilerParams(vmem_limit_bytes=32 << 20),
-    )(rows, root)
+        out_specs=whole(own.shape),
+        scratch_shapes=[
+            pltpu.VMEM((rows, columns), jnp.bfloat16),
+            pltpu.VMEM((rows, columns), jnp.float32),
+            pltpu.VMEM((rows, 1), jnp.float32),
+        ],
+        compiler_params=pltpu.CompilerParams(vmem_limit_bytes=40 << 20),
+    )(own, named, alive, root, blocks, keys)
 
 
 def by_gather(embeddings, owner_ids, live_mask):
@@ -235,10 +277,10 @@
         own, everyone, (((0,), (0,)), ((), ())), preferred_element_type=jnp.float32
     )
     moment = plane_gather(part, owners, 32, 2, True).reshape(columns, columns)
-    whitened = whiten_rows(everyone, root_of(moment), held)
-    mine = lax.dynamic_slice_in_dim(whitened, lax.axis_index("rows") * held, rows_here, 0)
-    alive = (live_mask > 0).astype(jnp.float32)
-    return masked_means(mine, whitened, owner_ids == keys[None, :], alive)
+    alive = (live_mask > 0).astype(jnp.float32)[:, None]
+    return join_rows(
+        embeddings, owner_ids, alive, root_of(moment), blocks, keys.reshape(owners, 1, held)
+    )
 
 
 def solution(mesh):

time: 212 us -> 202 us (0.953)
  matrix products: 45 us -> 23.9 us
  Pallas kernels: 146 us -> 163 us
  local copies, waits for them, and re-layouts: 11 us -> 6.82 us
    dot_general x2 -> x0, matrix products: 21.1 us -> none  [the longest x1 12.3 us: masked_means(): lax.dot_general(queries, members, (((1,), (1,)), ((), ())), preferred_ele...]
    pallas_call x1, Pallas kernels: 18.7 us -> 35.5 us  [join_rows(): pl.pallas_call(join_kernel, grid=(count,), out_shape=jax.ShapeDtypeStruct...]
    unnamed x7 -> x10, local copies, waits for them, and re-layouts: 10.9 us -> 6.58 us
where the time goes in v3:
time: 202 us
  Pallas kernels  163 us (81%)
  matrix products  23.9 us (12%)
  other arithmetic  8.28 us (4%)
  local copies, waits for them, and re-layouts  6.82 us (3%)
    pallas_call x2, Pallas kernels, plane_gather(): pl.pallas_call(functools.partial(gather_kernel, owners, reduced, chunks),...  127 us
    pallas_call x1, Pallas kernels, join_rows(): pl.pallas_call(join_kernel, grid=(count,), out_shape=jax.ShapeDtypeStruct...  35.5 us
    dot_general x1, matrix products, by_gather(): lax.dot_general(own, everyone, (((0,), (0,)), ((), ())), preferred_elemen...  8.52 us
    dot_general x1, matrix products, root_of(): jnp.dot(square, inner, precision=SPLIT)  7.84 us
    dot_general x1, matrix products, root_of(): square = jnp.dot(y, y, precision=SPLIT)  7.54 us
    unnamed x10, local copies, waits for them, and re-layouts  6.58 us

profile of v3, /device:TPU:0, one launch (start us, length us, event | category | flops | bytes accessed | tf_op | source)
XLA Modules:
  0.0 202.0 jit_solution(1196825774654926287)
XLA Ops:
  0.0 0.7 reduce.2
  0.7 0.7 select_convert_fusion
  1.4 1.2 fusion.7.refs_0_
  2.6 83.8 %shard_map.37.x_ref = bf16[16,368,1024]{2,1,0:T(8,128)(2,1)S(1)} custom-call(bf16[368,1024]{1,0:T(8,128)(2,1)S(1)} %fusion.7.refs_0_), custom_call_target="tpu_custom_call" | custom-call | tf_op jit(solution)/shard_map/pallas_call | solution.py:187
  86.3 0.0 copy-start
  86.3 4.5 %copy-done = bf16[16,368,1024]{2,1,0:T(8,128)(2,1)} copy-done((bf16[16,368,1024]{2,1,0:T(8,128)(2,1)}, bf16[16,368,1024]{2,1,0:T(8,128)(2,1)S(1)}, u32[]{:S(2)}) %copy-start) | copy-done | bytes 12058648
  90.8 0.1 reshape.28
  90.9 8.5 %fusion.3.refs_0_ = f32[64,1024]{1,0:T(8,128)S(1)} fusion(bf16[5888,1024]{1,0:T(8,128)(2,1)} %bitcast.20, s32[]{:T(128)S(6)} %select_n.8, bf16[5888]{0:T(1024)(128)(2,1)S(1)} %reshape.28), kind=kOutput, calls=%fused_computation.11 | convolution fusion | flops 773259264 | bytes 13839876 | tf_op jit(solution)/shard_map/dot_general | solution.py:276
  99.5 43.6 %shard_map.38 = f32[16,64,1024]{2,1,0:T(8,128)S(1)} custom-call(f32[64,1024]{1,0:T(8,128)S(1)} %fusion.3.refs_0_), custom_call_target="tpu_custom_call" | custom-call | tf_op jit(solution)/shard_map/pallas_call | solution.py:187
  143.1 0.0 copy-start.1
  143.1 2.0 copy-done.1
  145.1 0.4 abs_reduce_fusion
  145.5 0.6 reduce_max.9
  146.1 3.9 %broadcast_multiply_fusion = (f32[16,64,1024]{2,1,0:T(8,128)S(1)}, f32[16,64,1024]{2,1,0:T(8,128)S(1)}) fusion(f32[16,64,1024]{2,1,0:T(8,128)} %copy-done.1, f32[]{:T(128)} %reduce_max.9), kind=kLoop, calls=%fused_computation.7 | loop fusion | flops 2097152 | bytes 12582916 | tf_op jit(solution)/shard_map/mul | solution.py:38
  150.0 7.5 %fusion = (f32[1024,1024]{1,0:T(8,128)S(1)}, f32[1024,1024]{1,0:T(8,128)S(1)}) fusion(f32[16,64,1024]{2,1,0:T(8,128)S(1)} %get-tuple-element.5, f32[1024,1024]{1,0:T(8,128)S(1)} %bitcast.21), kind=kOutput, calls=%fused_computation.1 | convolution fusion | flops 6447693824 | bytes 16777216 | tf_op jit(solution)/shard_map/dot_general | solution.py:37
  157.5 0.8 broadcast_multiply_fusion.1
  158.3 0.0 copy-start.3
  158.4 0.0 copy-start.2
  158.4 7.8 %fusion.2.root_ref = bf16[1024,1024]{1,0:T(8,128)(2,1)S(1)} fusion(f32[16,64,1024]{2,1,0:T(8,128)S(1)} %broadcast_multiply_fusion.1, f32[1024,1024]{1,0:T(8,128)S(1)} %get-tuple-element.10, f32[1024,1024]{1,0:T(8,128)S(1)} %get-tuple-element.9), kind=kOutput, calls=%fused_computation.4 | convolution fusion | flops 6447693824 | bytes 14680064 | tf_op jit(solution)/shard_map/dot_general | solution.py:39
  166.3 0.1 reshape.29.alive_ref
  166.4 0.0 copy-done.3
  166.4 0.1 copy.10.named_ref
  166.5 0.0 copy-done.2
  166.5 35.5 %shard_map.39 = bf16[352,1024]{1,0:T(8,128)(2,1)} custom-call(bf16[352,1024]{1,0:T(8,128)(2,1)S(1)} %copy-done.2, s32[352,1]{1,0:T(8,128)S(1)} %copy.10.named_ref, f32[352,1]{1,0:T(8,128)S(1)} %reshape.29.alive_ref, bf16[1024,1024]{1,0:T(8,128)(2,1)S(1)} %fusion.2.root_ref, bf16[16,368,1024]{2,1,0:T(8,128)(2,1)} %copy-done, ...), custom_call_target="tpu_custom_call" | custom-call | tf_op jit(solution)/shard_map/pallas_call | solution.py:240
  (7 shorter events, 0.1 us)
Async XLA Ops:
  86.3 4.5 %copy-start = (bf16[16,368,1024]{2,1,0:T(8,128)(2,1)}, bf16[16,368,1024]{2,1,0:T(8,128)(2,1)S(1)}, u32[]{:S(2)}) copy-start(bf16[16,368,1024]{2,1,0:T(8,128)(2,1)S(1)} %shard_map.37.x_ref) | copy-start | bytes 36175876
  143.1 2.0 copy-start.1
  158.3 8.0 %copy-start.3 = (s32[352,1]{0,1:T(1,128)S(1)}, s32[352,1]{0,1:T(1,128)}, u32[]{:S(2)}) copy-start(s32[352,1]{0,1:T(1,128)} %param.4) | copy-start | bytes 4228
  158.4 8.2 %copy-start.2 = (bf16[352,1024]{1,0:T(8,128)(2,1)S(1)}, bf16[352,1024]{1,0:T(8,128)(2,1)}, u32[]{:S(2)}) copy-start(bf16[352,1024]{1,0:T(8,128)(2,1)} %own_ref.1) | copy-start | bytes 2162692

commit v4 on v3

--- a/solution.py
+++ b/solution.py
@@ -279,7 +279,7 @@
     moment = plane_gather(part, owners, 32, 2, True).reshape(columns, columns)
     alive = (live_mask > 0).astype(jnp.float32)[:, None]
     return join_rows(
-        embeddings, owner_ids, alive, root_of(moment), blocks, keys.reshape(owners, 1, held)
+        embeddings, owner_ids, alive, root_of(moment), blocks.reshape(owners // 2, 2 * held, columns), keys.reshape(owners // 2, 1, 2 * held)
     )
 
 

time: 202 us -> 198 us (0.980)
  Pallas kernels: 163 us -> 159 us
    pallas_call x1, Pallas kernels: 35.5 us -> 31.5 us  [join_rows(): pl.pallas_call(join_kernel, grid=(count,), out_shape=jax.ShapeDtypeStruct...]
where the time goes in v4:
time: 198 us
  Pallas kernels  159 us (80%)
  matrix products  23.9 us (12%)
  other arithmetic  8.28 us (4%)
  local copies, waits for them, and re-layouts  6.89 us (3%)
    pallas_call x2, Pallas kernels, plane_gather(): pl.pallas_call(functools.partial(gather_kernel, owners, reduced, chunks),...  127 us
    pallas_call x1, Pallas kernels, join_rows(): pl.pallas_call(join_kernel, grid=(count,), out_shape=jax.ShapeDtypeStruct...  31.5 us
    dot_general x1, matrix products, by_gather(): lax.dot_general(own, everyone, (((0,), (0,)), ((), ())), preferred_elemen...  8.52 us
    dot_general x1, matrix products, root_of(): jnp.dot(square, inner, precision=SPLIT)  7.84 us
    dot_general x1, matrix products, root_of(): square = jnp.dot(y, y, precision=SPLIT)  7.54 us
    unnamed x10, local copies, waits for them, and re-layouts  6.58 us

profile of v4, /device:TPU:0, one launch (start us, length us, event | category | flops | bytes accessed | tf_op | source)
XLA Modules:
  0.0 198.1 jit_solution(16232869832999623756)
XLA Ops:
  0.0 0.7 reduce.2
  0.7 0.7 select_convert_fusion
  1.4 1.2 fusion.7.refs_0_
  2.6 83.8 %shard_map.37 = bf16[16,368,1024]{2,1,0:T(8,128)(2,1)S(1)} custom-call(bf16[368,1024]{1,0:T(8,128)(2,1)S(1)} %fusion.7.refs_0_), custom_call_target="tpu_custom_call" | custom-call | tf_op jit(solution)/shard_map/pallas_call | solution.py:187
  86.3 0.0 copy-start
  86.3 4.5 %copy-done = bf16[16,368,1024]{2,1,0:T(8,128)(2,1)} copy-done((bf16[16,368,1024]{2,1,0:T(8,128)(2,1)}, bf16[16,368,1024]{2,1,0:T(8,128)(2,1)S(1)}, u32[]{:S(2)}) %copy-start) | copy-done | bytes 12058648
  90.8 0.1 reshape.32
  90.9 8.5 %fusion.3.refs_0_ = f32[64,1024]{1,0:T(8,128)S(1)} fusion(bf16[5888,1024]{1,0:T(8,128)(2,1)} %bitcast.21, s32[]{:T(128)S(6)} %select_n.8, bf16[5888]{0:T(1024)(128)(2,1)S(1)} %reshape.32), kind=kOutput, calls=%fused_computation.11 | convolution fusion | flops 773259264 | bytes 13839876 | tf_op jit(solution)/shard_map/dot_general | solution.py:276
  99.5 43.6 %shard_map.38 = f32[16,64,1024]{2,1,0:T(8,128)S(1)} custom-call(f32[64,1024]{1,0:T(8,128)S(1)} %fusion.3.refs_0_), custom_call_target="tpu_custom_call" | custom-call | tf_op jit(solution)/shard_map/pallas_call | solution.py:187
  143.1 0.0 copy-start.1
  143.1 2.0 copy-done.1
  145.1 0.4 abs_reduce_fusion
  145.5 0.6 reduce_max.9
  146.1 3.9 %broadcast_multiply_fusion = (f32[16,64,1024]{2,1,0:T(8,128)S(1)}, f32[16,64,1024]{2,1,0:T(8,128)S(1)}) fusion(f32[16,64,1024]{2,1,0:T(8,128)} %copy-done.1, f32[]{:T(128)} %reduce_max.9), kind=kLoop, calls=%fused_computation.7 | loop fusion | flops 2097152 | bytes 12582916 | tf_op jit(solution)/shard_map/mul | solution.py:38
  150.0 7.5 %fusion = (f32[1024,1024]{1,0:T(8,128)S(1)}, f32[1024,1024]{1,0:T(8,128)S(1)}) fusion(f32[16,64,1024]{2,1,0:T(8,128)S(1)} %get-tuple-element.5, f32[1024,1024]{1,0:T(8,128)S(1)} %bitcast.23), kind=kOutput, calls=%fused_computation.1 | convolution fusion | flops 6447693824 | bytes 16777216 | tf_op jit(solution)/shard_map/dot_general | solution.py:37
  157.5 0.8 broadcast_multiply_fusion.1
  158.3 0.0 copy-start.3
  158.4 0.0 copy-start.2
  158.4 7.8 %fusion.2.root_ref = bf16[1024,1024]{1,0:T(8,128)(2,1)S(1)} fusion(f32[16,64,1024]{2,1,0:T(8,128)S(1)} %broadcast_multiply_fusion.1, f32[1024,1024]{1,0:T(8,128)S(1)} %get-tuple-element.10, f32[1024,1024]{1,0:T(8,128)S(1)} %get-tuple-element.9), kind=kOutput, calls=%fused_computation.4 | convolution fusion | flops 6447693824 | bytes 14680064 | tf_op jit(solution)/shard_map/dot_general | solution.py:39
  166.2 0.1 reshape_reshape.3.key_ref
  166.3 0.1 reshape.33.alive_ref
  166.4 0.0 copy-done.3
  166.5 0.1 copy.7.named_ref
  166.6 0.0 copy-done.2
  166.6 31.5 %shard_map.39 = bf16[352,1024]{1,0:T(8,128)(2,1)} custom-call(bf16[352,1024]{1,0:T(8,128)(2,1)S(1)} %copy-done.2, s32[352,1]{1,0:T(8,128)S(1)} %copy.7.named_ref, f32[352,1]{1,0:T(8,128)S(1)} %reshape.33.alive_ref, bf16[1024,1024]{1,0:T(8,128)(2,1)S(1)} %fusion.2.root_ref, bf16[8,736,1024]{2,1,0:T(8,128)(2,1)} %bitcast.22, ...), custom_call_target="tpu_custom_call" | custom-call | tf_op jit(solution)/shard_map/pallas_call | solution.py:240
  (6 shorter events, 0.1 us)
Async XLA Ops:
  86.3 4.5 %copy-start = (bf16[16,368,1024]{2,1,0:T(8,128)(2,1)}, bf16[16,368,1024]{2,1,0:T(8,128)(2,1)S(1)}, u32[]{:S(2)}) copy-start(bf16[16,368,1024]{2,1,0:T(8,128)(2,1)S(1)} %shard_map.37) | copy-start | bytes 36175876
  143.1 2.0 copy-start.1
  158.3 8.1 %copy-start.3 = (s32[352,1]{0,1:T(1,128)S(1)}, s32[352,1]{0,1:T(1,128)}, u32[]{:S(2)}) copy-start(s32[352,1]{0,1:T(1,128)} %param.4) | copy-start | bytes 4228
  158.4 8.2 %copy-start.2 = (bf16[352,1024]{1,0:T(8,128)(2,1)S(1)}, bf16[352,1024]{1,0:T(8,128)(2,1)}, u32[]{:S(2)}) copy-start(bf16[352,1024]{1,0:T(8,128)(2,1)} %own_ref.1) | copy-start | bytes 2162692
